TPU v7x, 32 devices: a whole 2x2x4 slice. The times are simulated.
32 devices in a mesh: grp: 2 (over x), tm: 16 (over z, y, core).
Axes of the slice: x: 2, y: 2, z: 4, core: 2. Of those that a mesh axis runs over, the one named last changes fastest.
Arguments:
- right_sides: float32 [64, 4, 128], P(('grp', 'tm')), parts along dimension 0, may hold values from -6 to 6
- obs_var: float32 [64, 128], P(('grp', 'tm')), parts along dimension 0, may hold values from 0.25 to 1
- footprint: bfloat16 [512, 8, 128, 128], P(('grp', 'tm')), parts along dimension 0, may hold values from -0.5 to 0.5
- tile_block: int32 [512, 8], P(('grp', 'tm')), parts along dimension 0, may hold values from 0 to 1
- tile_place: int32 [512, 8], P(('grp', 'tm')), parts along dimension 0, may hold values from 0 to 1023
- time_cov: float32 [128, 128], replicated, as said below
- lat_cov: float32 [128, 128], replicated
- lon_cov: float32 [128, 128], replicated
Outputs:
- solution: float32 [64, 4, 128], P(('grp', 'tm')), parts along dimension 0
- flux_update: float32 [256, 128, 4, 128], P(('grp', 'tm')), parts along dimension 0
There are 2 independent parts, one for each index of `grp`. A program takes and returns all parts, laid end to end along the dimension named above; an argument that names none is the same for every part. Nothing has to cross between parts.
Inputs may be any that keep to these rules, and one draw needn't show every extreme that they name: time_cov, lat_cov and lon_cov are symmetric positive definite with positive entries.
All inputs are finite; a program needn't handle non-finite values.
Results may differ from a plain program's by a relative error of at most 0.0074.
Values may be sent and summed in bfloat16 or wider, within the bound.
No kernel may reach another device: no remote copies, remote signals or barrier semaphores. Data moves between devices by JAX's collectives and lax.ppermute only.
A program may use at most 64 MiB of HBM per device.

v0:
```python
import jax
import jax.numpy as jnp
from jax import lax
from jax.experimental import pallas as pl
from jax.experimental.pallas import tpu as pltpu
from jax.sharding import PartitionSpec as P

LAT = 128
LON = 128
BLOCK_OBS = 128
SAMPLES = 4
ITERS = 2


precise = lax.Precision.HIGHEST


def solve_spd(matrix, target):
    factor = jnp.linalg.cholesky(matrix)
    halfway = lax.linalg.triangular_solve(factor, target, left_side=True, lower=True)
    return lax.linalg.triangular_solve(
        factor, halfway, left_side=True, lower=True, transpose_a=True
    )


def combine(vectors, weights):
    return jnp.einsum("nks,kj->njs", vectors, weights, precision=precise)


def gram(left, right):
    return jnp.einsum("nks,njs->kj", left, right, precision=precise)


def to_all(array):
    devices = lax.axis_size("tm")
    copies = jnp.broadcast_to(array[None], (devices,) + array.shape)
    return lax.all_to_all(copies, "tm", split_axis=0, concat_axis=0, tiled=True)


def by_gather(
    right_sides, obs_var, footprint, tile_block, tile_place, time_cov, lat_cov, lon_cov
):
    devices = lax.axis_size("tm")
    me = lax.axis_index("tm")
    owned = right_sides.shape[0]
    blocks = devices * owned
    steps_here = time_cov.shape[0] // devices
    slots = tile_block.shape[1]
    tiles = devices * slots
    rows_here = steps_here * LAT
    owner_base = (jnp.arange(devices, dtype=jnp.int32) * owned)[:, None]
    requests = owner_base + tile_block

    packed = jnp.concatenate(
        [
            right_sides.reshape(-1, 128),
            obs_var.reshape(-1, 128),
            tile_place.astype(jnp.float32).reshape(-1, 128),
        ]
    )
    everyone = to_all(packed)
    at = owned * SAMPLES
    rhs = everyone[:, :at].reshape(blocks, SAMPLES, BLOCK_OBS)
    variance = everyone[:, at : at + owned].reshape(blocks, BLOCK_OBS)
    places = everyone[:, at + owned :].reshape(devices, tiles).astype(jnp.int32)
    times = (places // LAT + steps_here * jnp.arange(devices, dtype=jnp.int32)[:, None]).reshape(-1)
    rows = (places % LAT).reshape(-1)
    time_hot = (jnp.arange(time_cov.shape[0])[:, None] == times[None, :]).astype(jnp.float32)
    row_hot = (jnp.arange(LAT)[:, None] == rows[None, :]).astype(jnp.float32)
    my_times = lax.dynamic_slice_in_dim(time_cov, me * steps_here, steps_here, 0)
    time_part = jnp.dot(my_times, time_hot, precision=precise)
    row_part = jnp.dot(lat_cov, row_hot, precision=precise)
    dense = (time_part[:, None, :] * row_part[None, :, :]).astype(jnp.bfloat16)
    dense = dense.reshape(rows_here, devices * tiles)
    mine = jnp.take(dense, tile_place.reshape(-1), axis=0)

    def spread(vectors):
        chosen = jnp.take(vectors.astype(jnp.bfloat16), requests, axis=0)
        contrib = jnp.einsum(
            "ocks,ocsl->ockl", chosen, footprint, preferred_element_type=jnp.float32
        )
        contrib = contrib.astype(jnp.bfloat16).reshape(tiles, SAMPLES * LON)
        return lax.all_gather(contrib, "tm", axis=0, tiled=True)

    def collect(gathered):
        field = jnp.dot(mine, gathered, preferred_element_type=jnp.float32)
        field = jnp.dot(field.reshape(-1, LON), lon_cov, precision=precise)
        picked = field.astype(jnp.bfloat16).reshape(devices, slots, SAMPLES, LON)
        partial = jnp.einsum(
            "ockl,ocsl->ocks", picked, footprint, preferred_element_type=jnp.float32
        )
        block_range = jnp.arange(owned, dtype=jnp.int32)
        selector = (tile_block[:, :, None] == block_range).astype(jnp.float32)
        summed = jnp.einsum("ocb,ocks->obks", selector, partial, precision=precise)
        terms = lax.all_to_all(
            summed.reshape(devices, owned * SAMPLES, BLOCK_OBS), "tm", 0, 0, tiled=True
        )
        return to_all(terms.sum(0)).reshape(blocks, SAMPLES, BLOCK_OBS)

    solution = jnp.zeros_like(rhs)
    residual = rhs
    direction = rhs
    norm_now = gram(rhs, rhs)
    gathers, sizes = [], []
    for step in range(ITERS):
        gathered = spread(direction)
        image = collect(gathered) + variance[:, None, :] * direction
        step_size = solve_spd(gram(direction, image), norm_now)
        gathers.append(gathered)
        sizes.append(step_size)
        solution = solution + combine(direction, step_size)
        if step + 1 == ITERS:
            break
        residual = residual - combine(image, step_size)
        norm_next = gram(residual, residual)
        mix_ratio = solve_spd(norm_now, norm_next)
        direction = residual + combine(direction, mix_ratio)
        norm_now = norm_next

    def mix(gathered, size):
        whole = gathered.astype(jnp.float32).reshape(-1, SAMPLES, LON)
        return jnp.einsum("tkl,kj->tjl", whole, size, precision=precise)

    def apply_dense(gathered):
        return jnp.dot(dense, gathered, preferred_element_type=jnp.float32)

    if rows_here < devices * tiles // 4:
        flux = sum(mix(apply_dense(g), size) for g, size in zip(gathers, sizes))
    else:
        total = sum(mix(g, size) for g, size in zip(gathers, sizes))
        flux = apply_dense(total.astype(jnp.bfloat16).reshape(-1, SAMPLES * LON))
    flux = jnp.dot(flux.reshape(-1, LON), lon_cov, precision=precise)
    mine_now = lax.dynamic_slice_in_dim(solution, me * owned, owned, 0)
    return (mine_now, flux.reshape(steps_here, LAT, SAMPLES, LON))


def rolled(x, shift):
    return x if shift == 0 else pltpu.roll(x, 8 - 2 * shift, x.ndim - 2)


def row_gram(left, right):
    entry = [[None] * SAMPLES for _ in range(SAMPLES)]
    for shift in range(SAMPLES):
        product = jnp.sum(left * rolled(right, shift), axis=0)
        total = jnp.broadcast_to(jnp.sum(product, axis=1, keepdims=True), product.shape)
        for k in range(SAMPLES):
            pair = total[2 * k : 2 * k + 1] + total[2 * k + 1 : 2 * k + 2]
            entry[k][(k + shift) % SAMPLES] = pair
    return entry


def row_solve(matrix, target):
    size = range(SAMPLES)
    sym = [[0.5 * (matrix[i][j] + matrix[j][i]) for j in size] for i in size]
    low = [[None] * SAMPLES for _ in size]
    scaled = [[None] * SAMPLES for _ in size]
    inverse = []
    for j in size:
        pivot = sym[j][j]
        for p in range(j):
            pivot = pivot - low[j][p] * scaled[j][p]
        inverse.append(1.0 / pivot)
        for i in range(j + 1, SAMPLES):
            value = sym[i][j]
            for p in range(j):
                value = value - scaled[i][p] * low[j][p]
            scaled[i][j] = value
            low[i][j] = value * inverse[j]
    out = [[None] * SAMPLES for _ in size]
    for c in size:
        part = []
        for i in size:
            value = target[i][c]
            for p in range(i):
                value = value - low[i][p] * part[p]
            part.append(value)
        for i in reversed(size):
            value = part[i] * inverse[i]
            for p in range(i + 1, SAMPLES):
                value = value - low[p][i] * out[p][c]
            out[i][c] = value
    return out


def row_weights(weights):
    sample = lax.broadcasted_iota(jnp.int32, (8, 128), 0) // 2
    result = []
    for shift in range(SAMPLES):
        rows = jnp.broadcast_to(weights[shift][0], (8, 128))
        for j in range(1, SAMPLES):
            rows = jnp.where(sample == j, weights[(j + shift) % SAMPLES][j], rows)
        result.append(rows)
    return result


def row_combine(x, per_shift):
    total = 0.0
    for shift in range(SAMPLES):
        total = total + rolled(x, shift) * per_shift[shift]
    return total


PIECES = 8


def fetch(source, held, arrived):
    pieces = arrived.shape[0]
    size = source.shape[0] // pieces
    copies = []
    for p in range(pieces):
        at = pl.ds(p * size, size)
        copies.append(pltpu.make_async_copy(source.at[at], held.at[at], arrived.at[p]))
    for copy in copies:
        copy.start()
    return copies


def second_of(tile_block):
    slots, owners = tile_block.shape
    tiles = owners * slots
    tile = lax.broadcasted_iota(jnp.int32, (tiles, slots), 0)
    slot = lax.broadcasted_iota(jnp.int32, (tiles, slots), 1)
    rows = jnp.dot(
        (tile % slots == slot).astype(jnp.float32),
        tile_block[...].astype(jnp.float32),
        preferred_element_type=jnp.float32,
    )
    tile = lax.broadcasted_iota(jnp.int32, (tiles, owners), 0)
    owner = lax.broadcasted_iota(jnp.int32, (tiles, owners), 1)
    return jnp.sum(jnp.where(tile // slots == owner, rows, 0.0), axis=1, keepdims=True) > 0.5


def pack_body(right_sides, obs_var, tile_place, copies):
    slots, owners = tile_place.shape
    tiles = owners * slots
    owner = lax.broadcasted_iota(jnp.int32, (owners, tiles), 0)
    lane = lax.broadcasted_iota(jnp.int32, (owners, tiles), 1)
    spread_out = jnp.dot(
        tile_place[...].astype(jnp.float32),
        (lane // slots == owner).astype(jnp.float32),
        precision=precise,
        preferred_element_type=jnp.float32,
    )
    slot = lax.broadcasted_iota(jnp.int32, (slots, tiles), 0)
    lane = lax.broadcasted_iota(jnp.int32, (slots, tiles), 1)
    place = jnp.sum(jnp.where(lane % slots == slot, spread_out, 0.0), axis=0, keepdims=True)
    for k in range(SAMPLES):
        for b in range(2):
            copies[0, 2 * k + b : 2 * k + b + 1] = right_sides[b, k : k + 1]
    copies[0, 8:10] = obs_var[...]
    copies[0, 10:11] = place
    copies[0, 11:16] = jnp.zeros((5, tiles), jnp.float32)
    for d in range(1, copies.shape[0]):
        copies[d] = copies[0]


def spread_tiles(vectors, held, copies, products, split):
    owners, slots = held.shape[:2]
    for owner in range(owners):
        if owner % (owners // PIECES) == 0:
            copies[owner // (owners // PIECES)].wait()
        rows = vectors[owner, 0:8]
        lhs = rows.astype(jnp.bfloat16)
        if split:
            upper = lhs.astype(jnp.float32)
            lhs = jnp.concatenate([upper, rows - upper], axis=0).astype(jnp.bfloat16)
        for c in range(slots):
            r = jnp.dot(lhs, held[owner, c], preferred_element_type=jnp.float32)
            products[owner * slots + c] = r[:8] + r[8:] if split else r


def spread_end(products, second, lon, by_column, by_tile):
    width = by_column.shape[1]
    chunks = LON // width
    for k in range(SAMPLES):
        chosen = jnp.where(second, products[:, 2 * k + 1, :], products[:, 2 * k, :])
        mixed = jnp.dot(
            chosen, lon[...], precision=precise, preferred_element_type=jnp.float32
        )
        by_tile[:, k * LON : (k + 1) * LON] = mixed.astype(jnp.bfloat16)
        turned = mixed.T.astype(jnp.bfloat16)
        by_column[k * chunks : (k + 1) * chunks] = turned.reshape(chunks, width, LON)


def first_body(
    everyone, tile_block, lon, footprint, by_column, by_tile, products, held, arrived
):
    copies = fetch(footprint, held, arrived)
    spread_tiles(everyone, held, copies, products, False)
    spread_end(products, second_of(tile_block), lon, by_column, by_tile)


def with_variance(image, everyone, vectors):
    block = lax.broadcasted_iota(jnp.int32, vectors.shape, 1) % 2
    variance = jnp.where(block == 0, everyone[:, 8:9, :], everyone[:, 9:10, :])
    return image + variance * vectors


def entries(ref):
    grid = range(SAMPLES)
    return [[ref[SAMPLES * k + j : SAMPLES * k + j + 1] for j in grid] for k in grid]


def keep(ref, matrix):
    for k in range(SAMPLES):
        for j in range(SAMPLES):
            ref[SAMPLES * k + j : SAMPLES * k + j + 1] = matrix[k][j]


def update_body(
    everyone, image_in, tile_block, lon, footprint,
    by_column, by_tile, direction, sizes, norm, products, held, arrived,
):
    copies = fetch(footprint, held, arrived)
    first = everyone[:, 0:8, :]
    image = with_variance(image_in[...], everyone, first)
    norm_now = row_gram(first, first)
    step_size = row_solve(row_gram(first, image), norm_now)
    residual = first - row_combine(image, row_weights(step_size))
    norm_next = row_gram(residual, residual)
    ratio = row_solve(norm_now, norm_next)
    direction[...] = residual + row_combine(first, row_weights(ratio))
    keep(sizes, step_size)
    keep(norm, norm_next)
    spread_tiles(direction, held, copies, products, True)
    spread_end(products, second_of(tile_block), lon, by_column, by_tile)


def build_body(
    me, everyone, time_cov, lat_cov, tile_prior, time_part, row_part, hot, cols, times
):
    devices, tiles = everyone.shape[0], everyone.shape[2]
    steps_here = time_part.shape[0]
    rows = tile_prior.shape[0]
    step = pl.program_id(0)

    @pl.when(step == 0)
    def _():
        at = lax.broadcasted_iota(jnp.int32, (LAT, tiles), 0)
        for kind, cov in ((0, time_cov), (1, lat_cov)):
            whole_cov = cov[...]
            upper = whole_cov.astype(jnp.bfloat16)
            lower = (whole_cov - upper.astype(jnp.float32)).astype(jnp.bfloat16)
            ones = []
            for d in range(devices):
                place = (everyone[d, 10:11, :] + 0.5).astype(jnp.int32)
                where = place // LAT + steps_here * d if kind == 0 else place % LAT
                one = (at == where).astype(jnp.float32)
                ones.append(one.astype(jnp.bfloat16))
                turned = one.T.astype(jnp.bfloat16)
                here = slice(d * tiles, (d + 1) * tiles)
                hot[kind, here, 0:LAT] = turned
                hot[kind, here, LAT : 2 * LAT] = turned
            picked = jnp.dot(
                jnp.concatenate([upper, lower], axis=0),
                jnp.concatenate(ones, axis=1),
                preferred_element_type=jnp.float32,
            )
            cols[kind] = picked.astype(jnp.bfloat16)
            both = picked[:LAT] + picked[LAT:]
            if kind == 0:
                times[...] = both
                mine = pl.ds(pl.multiple_of(me[0] * steps_here, steps_here), steps_here)
                time_part[...] = times[mine, :]
            else:
                row_part[...] = both

    block = pl.ds(pl.multiple_of(step * rows, rows), rows)
    by_time = jnp.dot(hot[0, block, :], cols[0], preferred_element_type=jnp.float32)
    by_row = jnp.dot(hot[1, block, :], cols[1], preferred_element_type=jnp.float32)
    tile_prior[...] = (by_time * by_row).astype(jnp.bfloat16)


def mix_body(columns, tile_prior, mixed, total, held, arrived):
    copies = fetch(tile_prior, held, arrived)
    devices, width, tiles = columns.shape
    part = devices // len(copies)
    for p, copy in enumerate(copies):
        at = range(p * part, (p + 1) * part)
        lhs = jnp.concatenate([columns[d] for d in at], axis=1)
        copy.wait()
        product = jnp.dot(
            lhs,
            held[p * part * tiles : (p + 1) * part * tiles],
            preferred_element_type=jnp.float32,
        )
        total[...] = product if p == 0 else total[...] + product
    for d in range(devices):
        mixed[d] = total[:, d * tiles : (d + 1) * tiles].astype(jnp.bfloat16)


def collect_body(values, tile_block, footprint, *rest):
    sums, rows = rest[-2:]
    chunks = values.shape[0] // SAMPLES
    owners, slots = footprint.shape[:2]
    is_second = second_of(tile_block)
    for k in range(SAMPLES):
        turned = values[k * chunks : (k + 1) * chunks].reshape(LON, -1)
        turned = turned.astype(jnp.float32).T
        rows[:, 2 * k, :] = jnp.where(is_second, 0.0, turned)
        rows[:, 2 * k + 1, :] = jnp.where(is_second, turned, 0.0)
    for owner in range(owners):
        total = 0.0
        for c in range(slots):
            total = total + lax.dot_general(
                rows[owner * slots + c].astype(jnp.bfloat16),
                footprint[owner, c],
                (((1,), (1,)), ((), ())),
                preferred_element_type=jnp.float32,
            )
        sums[owner] = total


def apply_flux(time_part, row_part, source, out):
    steps = time_part.shape[0]
    pair = 2
    for step in range(0, steps, pair):
        dense = []
        for t in range(step, step + pair):
            dense.append((time_part[t : t + 1, :] * row_part[...]).astype(jnp.bfloat16))
        out[step * LAT : (step + pair) * LAT] = jnp.dot(
            jnp.concatenate(dense, axis=0), source[...], preferred_element_type=jnp.float32
        )


def flux_first_body(
    sizes, time_part, row_part, gathered,
    out, token, rows, held, total, row_arrived, arrived,
):
    copies = fetch(gathered, held, arrived)
    row_copies = fetch(row_part, rows, row_arrived)
    size = entries(sizes)
    part = total.shape[0] // len(copies)
    for r, copy in enumerate(copies):
        copy.wait()
        at = slice(r * part, (r + 1) * part)
        for j in range(SAMPLES):
            value = 0.0
            for k in range(SAMPLES):
                piece = held[at, k * LON : (k + 1) * LON]
                value = value + piece.astype(jnp.float32) * size[k][j]
            total[at, j * LON : (j + 1) * LON] = value.astype(jnp.bfloat16)
    for copy in row_copies:
        copy.wait()
    apply_flux(time_part, rows, total, out)
    token[...] = out[0:8, 0:128]


def flux_second_body(
    after, time_part, row_part, gathered, out, rows, held, row_arrived, arrived
):
    del after
    row_copies = fetch(row_part, rows, row_arrived)
    copies = fetch(gathered, held, arrived)
    for copy in row_copies + copies:
        copy.wait()
    apply_flux(time_part, rows, held, out)


def last_body(
    me, everyone, image_in, direction, sizes, norm, flux_one, flux_two,
    answer, flux, last_size,
):
    @pl.when(pl.program_id(0) == 0)
    def _():
        second = direction[...]
        image = with_variance(image_in[...], everyone, second)
        size_two = row_solve(row_gram(second, image), entries(norm))
        keep(last_size, size_two)
        own = row_combine(everyone[me[0], 0:8, :], row_weights(entries(sizes)))
        own = own + row_combine(direction[me[0]], row_weights(size_two))
        for k in range(SAMPLES):
            for b in range(2):
                answer[b, k : k + 1, :] = own[2 * k + b : 2 * k + b + 1]

    size_two = entries(last_size)
    for t in range(flux.shape[0]):
        at = slice(t * LAT, (t + 1) * LAT)
        parts = [flux_two[at, k * LON : (k + 1) * LON] for k in range(SAMPLES)]
        for j in range(SAMPLES):
            value = flux_one[at, j * LON : (j + 1) * LON]
            for k in range(SAMPLES):
                value = value + parts[k] * size_two[k][j]
            flux[t, :, j, :] = value


def whole(shape):
    return pl.BlockSpec(shape, lambda i, *_: (0,) * len(shape))


MIB = 1024 * 1024


def params(grant=59):
    return pltpu.CompilerParams(vmem_limit_bytes=grant * MIB)


def shape_of(shape, dtype):
    return jax.ShapeDtypeStruct(shape, dtype)


def cost(flops, moved):
    return pl.CostEstimate(flops=flops, bytes_accessed=moved, transcendentals=0)


def by_columns(
    right_sides, obs_var, footprint, tile_block, tile_place, time_cov, lat_cov, lon_cov
):
    devices = lax.axis_size("tm")
    me = lax.axis_index("tm").reshape(1).astype(jnp.int32)
    steps_here = time_cov.shape[0] // devices
    tiles = tile_block.size
    every_tile = devices * tiles
    columns = SAMPLES * LON
    width = columns // devices
    rows_here = steps_here * LAT
    f32, bf16 = jnp.float32, jnp.bfloat16

    vmem = pl.BlockSpec(memory_space=pltpu.VMEM)
    smem = pl.BlockSpec(memory_space=pltpu.SMEM)
    hbm = pl.BlockSpec(memory_space=pltpu.HBM)
    vector_shape = shape_of((devices, 8, BLOCK_OBS), f32)
    column_shape = shape_of((devices, width, tiles), bf16)
    tile_shape = shape_of((tiles, columns), bf16)
    small_shape = shape_of((SAMPLES * SAMPLES, 128), f32)
    field_shape = shape_of((rows_here, columns), f32)
    turned_block = tile_block.T
    row_shape = shape_of((LAT, every_tile), f32)
    row_scratch = [pltpu.VMEM(row_shape.shape, f32)]
    held_scratch = [pltpu.VMEM((every_tile, columns), bf16)]
    copied = [pltpu.SemaphoreType.DMA((1,)), pltpu.SemaphoreType.DMA((PIECES,))]
    tile_scratch = [
        pltpu.VMEM((tiles, 8, LON), f32),
        pltpu.VMEM(footprint.shape, bf16),
        pltpu.SemaphoreType.DMA((PIECES,)),
    ]
    tile_cost = cost(2 * 8 * footprint.size, footprint.size * 2)
    flux_cost = cost(2 * rows_here * every_tile * columns, every_tile * columns * 2)

    def call(body, in_specs, out_shape, scratch, estimate, name, grant=59):
        specs = [vmem] * len(out_shape) if isinstance(out_shape, list) else vmem
        return pl.pallas_call(
            body,
            in_specs=in_specs,
            out_specs=specs,
            out_shape=out_shape,
            scratch_shapes=scratch,
            compiler_params=params(grant),
            cost_estimate=estimate,
            name=name,
        )

    def exchange(array):
        return lax.all_to_all(array, "tm", split_axis=0, concat_axis=0, tiled=True)

    packed_shape = shape_of((devices, 16, 128), f32)
    everyone = exchange(
        call(pack_body, [vmem] * 3, packed_shape, [], cost(0, 1 << 17), "pack")(
            right_sides, obs_var, tile_place.T
        )
    )
    by_column, by_tile = call(
        first_body,
        [vmem, vmem, vmem, hbm],
        [column_shape, tile_shape],
        tile_scratch,
        tile_cost,
        "spread_first",
    )(everyone, turned_block, lon_cov, footprint)
    gathered_one = lax.all_gather(by_tile, "tm", axis=0, tiled=True)

    build_rows = every_tile // 8
    tile_prior, time_part, row_part = pl.pallas_call(
        build_body,
        grid=(8,),
        in_specs=[
            smem,
            whole(everyone.shape),
            whole(time_cov.shape),
            whole(lat_cov.shape),
        ],
        out_specs=[
            pl.BlockSpec((build_rows, every_tile), lambda i: (i, 0)),
            whole((steps_here, every_tile)),
            whole(row_shape.shape),
        ],
        out_shape=[
            shape_of((every_tile, every_tile), bf16),
            shape_of((steps_here, every_tile), f32),
            row_shape,
        ],
        scratch_shapes=[
            pltpu.VMEM((2, every_tile, 2 * LAT), bf16),
            pltpu.VMEM((2, 2 * LAT, every_tile), bf16),
            pltpu.VMEM((LAT, every_tile), f32),
        ],
        compiler_params=params(),
        cost_estimate=cost(4 * every_tile * every_tile * 256, every_tile * every_tile * 2),
        name="build_prior",
    )(me, everyone, time_cov, lat_cov)

    def prior(by_column):
        mixed = call(
            mix_body,
            [vmem, hbm],
            column_shape,
            [
                pltpu.VMEM((width, every_tile), f32),
                pltpu.VMEM((every_tile, every_tile), bf16),
                pltpu.SemaphoreType.DMA((PIECES,)),
            ],
            cost(2 * width * every_tile**2, every_tile**2 * 2),
            "mix_columns",
        )(exchange(by_column), tile_prior)
        return exchange(mixed)

    def collect(values, *after):
        sums = call(
            collect_body,
            [vmem] * 3 + [hbm] * len(after),
            vector_shape,
            tile_scratch[:1],
            tile_cost,
            "collect",
            48,
        )(values, turned_block, footprint, *after)
        return exchange(sums).sum(0)

    image = to_all(collect(prior(by_column)))
    by_column, by_tile, direction, sizes, norm = call(
        update_body,
        [vmem] * 4 + [hbm],
        [column_shape, tile_shape, vector_shape, small_shape, small_shape],
        tile_scratch,
        tile_cost,
        "update_spread",
    )(everyone, image, turned_block, lon_cov, footprint)
    gathered_two = lax.all_gather(by_tile, "tm", axis=0, tiled=True)
    flux_one, token = call(
        flux_first_body,
        [vmem, vmem, hbm, hbm],
        [field_shape, shape_of((8, 128), f32)],
        row_scratch + held_scratch * 2 + copied,
        flux_cost,
        "flux_first",
    )(sizes, time_part, row_part, gathered_one)

    own_image = collect(prior(by_column), token)
    image = to_all(own_image)
    flux_two = call(
        flux_second_body,
        [hbm, vmem, hbm, hbm],
        field_shape,
        row_scratch + held_scratch + copied,
        flux_cost,
        "flux_second",
    )(own_image, time_part, row_part, gathered_two)

    stages = 4
    block = pl.BlockSpec((rows_here // stages, columns), lambda i: (i, 0))
    answer, flux = pl.pallas_call(
        last_body,
        grid=(stages,),
        in_specs=[
            smem,
            whole(everyone.shape),
            whole(image.shape),
            whole(direction.shape),
            whole(sizes.shape),
            whole(norm.shape),
            block,
            block,
        ],
        out_specs=[
            whole(right_sides.shape),
            pl.BlockSpec((steps_here // stages, LAT, SAMPLES, LON), lambda i: (i, 0, 0, 0)),
        ],
        out_shape=[
            shape_of(right_sides.shape, f32),
            shape_of((steps_here, LAT, SAMPLES, LON), f32),
        ],
        scratch_shapes=[pltpu.VMEM(small_shape.shape, f32)],
        compiler_params=params(),
        cost_estimate=cost(1 << 20, 6 << 20),
        name="last",
    )(me, everyone, image, direction, sizes, norm, flux_one, flux_two)
    return (answer, flux)


def local(right_sides, obs_var, footprint, tile_block, tile_place, *covariances):
    devices = lax.axis_size("tm")
    tiles = tile_block.size
    fits = devices * tiles <= 2048 and devices % 4 == 0 and tiles == 128
    fits = fits and right_sides.shape[0] == 2 and (SAMPLES * LON) % (32 * devices) == 0
    fits = fits and (covariances[0].shape[0] // devices) % 4 == 0
    plan = by_columns if fits else by_gather
    return plan(right_sides, obs_var, footprint, tile_block, tile_place, *covariances)


def solution(mesh):
    in_specs = (
        P(("grp", "tm"), None, None),
        P(("grp", "tm"), None),
        P(("grp", "tm"), None, None, None),
        P(("grp", "tm"), None),
        P(("grp", "tm"), None),
        P(),
        P(),
        P(),
    )
    out_specs = (P(("grp", "tm"), None, None), P(("grp", "tm"), None, None, None))
    return jax.shard_map(local, mesh=mesh, in_specs=in_specs, out_specs=out_specs, check_vma=False)
```

profile of v0, /device:TPU:0, one launch (start us, length us, event | category | flops | bytes accessed | tf_op | source)
XLA Modules:
  0.0 165.2 jit_solution(2466672973696242680)
XLA Ops:
  7.2 0.0 all-gather.3.cloned.1.call-start
  7.2 1.5 pack.1
  8.7 15.4 %all_to_all.45.everyone = f32[16,16,128]{2,1,0:T(8,128)} all-to-all(f32[16,16,128]{2,1,0:T(8,128)} %pack.1), channel_id=1, replica_groups=mesh['grp'=2,'tm'=16] {'tm'}, dimensions={0} | all-to-all | bytes 262144 | tf_op jit(solution)/shard_map/all_to_all | solution.py:554
  24.2 5.4 %spread_first.1 = (bf16[16,32,128]{2,1,0:T(8,128)(2,1)}, bf16[128,512]{1,0:T(8,128)(2,1)}) custom-call(f32[16,16,128]{2,1,0:T(8,128)} %all_to_all.45.everyone, s32[8,16]{1,0:T(8,128)} %bitcast.3, f32[128,128]{1,0:T(8,128)} %lon.3, bf16[16,8,128,128]{3,2,1,0:T(8,128)(2,1)} %footprint.7), custom_call_target="tpu_custom_call" | custom-call | flops 33554432 | bytes 4194304 | tf_op jit(solution)/shard_map/spread_first/pallas_call | solution.py:562
  29.6 0.0 all-gather.3.cloned.1.call-update
  29.6 3.5 %all-to-all-start.1 = ((bf16[16,32,128]{2,1,0:T(8,128)(2,1)}), bf16[16,32,128]{2,1,0:T(8,128)(2,1)S(1)}, u32[]{:S(2)}, u32[]{:S(2)}) async-start(bf16[16,32,128]{2,1,0:T(8,128)(2,1)} %get-tuple-element.14), calls=%async_computation.1 | async-start | bytes 262144 | tf_op jit(solution)/shard_map/all_to_all | solution.py:554
  33.1 0.0 all-gather.5.cloned.1.call-start
  33.2 9.8 %build_prior.1 = (bf16[2048,2048]{1,0:T(8,128)(2,1)}, f32[8,2048]{1,0:T(8,128)}, f32[128,2048]{1,0:T(8,128)}) custom-call(s32[1]{0:T(128)} %bitcast.me, f32[16,16,128]{2,1,0:T(8,128)} %all_to_all.45.everyone, f32[128,128]{1,0:T(8,128)} %time_cov.1, f32[128,128]{1,0:T(8,128)} %lat_cov.1), custom_call_target="tpu_custom_call" | custom-call | flops 4294967296 | bytes 8388608 | tf_op jit(solution)/shard_map/build_prior/pallas_call | solution.py:573
  42.9 0.0 all-to-all-done.1.columns
  42.9 0.0 copy-start.5
  42.9 0.6 copy-done.5
  43.6 0.0 copy-start
  43.6 0.0 copy-start.2
  43.6 5.8 %mix_columns.2 = bf16[16,32,128]{2,1,0:T(8,128)(2,1)} custom-call(bf16[16,32,128]{2,1,0:T(8,128)(2,1)} %copy-done.5, bf16[2048,2048]{1,0:T(8,128)(2,1)} %get-tuple-element.15.tile_prior), custom_call_target="tpu_custom_call" | custom-call | flops 268435456 | bytes 8388608 | tf_op jit(solution)/shard_map/mix_columns/pallas_call | solution.py:603
  49.4 15.5 %all_to_all.46.values = bf16[16,32,128]{2,1,0:T(8,128)(2,1)S(1)} all-to-all(bf16[16,32,128]{2,1,0:T(8,128)(2,1)} %mix_columns.2), channel_id=1, replica_groups=mesh['grp'=2,'tm'=16] {'tm'}, dimensions={0} | all-to-all | bytes 262144 | tf_op jit(solution)/shard_map/all_to_all | solution.py:554
  64.9 0.0 copy-done
  64.9 0.0 copy-done.2
  64.9 2.6 %collect.2 = f32[16,8,128]{2,1,0:T(8,128)S(1)} custom-call(bf16[16,32,128]{2,1,0:T(8,128)(2,1)S(1)} %all_to_all.46.values, s32[8,16]{1,0:T(8,128)S(1)} %bitcast.5, bf16[16,8,128,128]{3,2,1,0:T(8,128)(2,1)S(1)} %copy-done), custom_call_target="tpu_custom_call" | custom-call | flops 33554432 | bytes 4194304 | tf_op jit(solution)/shard_map/collect/pallas_call | solution.py:618
  67.5 10.4 %all_to_all.47 = f32[16,8,128]{2,1,0:T(8,128)S(1)} all-to-all(f32[16,8,128]{2,1,0:T(8,128)S(1)} %collect.2), channel_id=1, replica_groups=mesh['grp'=2,'tm'=16] {'tm'}, dimensions={0} | all-to-all | bytes 131072 | tf_op jit(solution)/shard_map/all_to_all | solution.py:554
  77.9 10.2 %all_to_all.48.image_in = f32[16,8,128]{2,1,0:T(8,128)} all-to-all(f32[16,8,128]{2,1,0:T(8,128)S(1)} %broadcast_in_dim.4), channel_id=1, replica_groups=mesh['grp'=2,'tm'=16] {'tm'}, dimensions={0} | all-to-all | bytes 131072 | tf_op jit(solution)/shard_map/all_to_all | solution.py:37
  88.1 5.4 %update_spread.1 = (bf16[16,32,128]{2,1,0:T(8,128)(2,1)}, bf16[128,512]{1,0:T(8,128)(2,1)}, f32[16,8,128]{2,1,0:T(8,128)}, f32[16,128]{1,0:T(8,128)}, f32[16,128]{1,0:T(8,128)}) custom-call(f32[16,16,128]{2,1,0:T(8,128)} %all_to_all.45.everyone, f32[16,8,128]{2,1,0:T(8,128)} %all_to_all.48.image_in, s32[8,16]{1,0:T(8,128)} %bitcast.4, f32[128,128]{1,0:T(8,128)} %lon.3, ...), custom_call_target="tpu_custom_call" | custom-call | flops 33554432 | bytes 4194304 | tf_op jit(solution)/shard_map/update_spread/pallas_call | solution.py:630
  93.5 0.0 all-gather.5.cloned.1.call-update
  93.6 13.6 %all_to_all.49.columns = bf16[16,32,128]{2,1,0:T(8,128)(2,1)} all-to-all(bf16[16,32,128]{2,1,0:T(8,128)(2,1)} %get-tuple-element.16), channel_id=1, replica_groups=mesh['grp'=2,'tm'=16] {'tm'}, dimensions={0} | all-to-all | bytes 262144 | tf_op jit(solution)/shard_map/all_to_all | solution.py:554
  107.2 5.3 %mix_columns.3 = bf16[16,32,128]{2,1,0:T(8,128)(2,1)} custom-call(bf16[16,32,128]{2,1,0:T(8,128)(2,1)} %all_to_all.49.columns, bf16[2048,2048]{1,0:T(8,128)(2,1)} %get-tuple-element.15.tile_prior), custom_call_target="tpu_custom_call" | custom-call | flops 268435456 | bytes 8388608 | tf_op jit(solution)/shard_map/mix_columns/pallas_call | solution.py:603
  112.5 3.7 %all-to-all-start.6 = ((bf16[16,32,128]{2,1,0:T(8,128)(2,1)}), bf16[16,32,128]{2,1,0:T(8,128)(2,1)S(1)}, u32[]{:S(2)}, u32[]{:S(2)}) async-start(bf16[16,32,128]{2,1,0:T(8,128)(2,1)} %mix_columns.3), calls=%async_computation.6 | async-start | bytes 262144 | tf_op jit(solution)/shard_map/all_to_all | solution.py:554
  116.2 0.0 all-gather.3.cloned.1.call-done.gathered
  116.2 0.0 copy-start.3
  116.2 7.2 %flux_first.1 = (f32[1024,512]{1,0:T(8,128)}, f32[8,128]{1,0:T(8,128)}) custom-call(f32[16,128]{1,0:T(8,128)} %get-tuple-element.17.sizes, f32[8,2048]{1,0:T(8,128)} %get-tuple-element.18.time_part, f32[128,2048]{1,0:T(8,128)} %get-tuple-element.19.row_part, bf16[2048,512]{1,0:T(8,128)(2,1)} %all-gather.3.cloned.1.call-done.gathered), custom_call_target="tpu_custom_call" | custom-call | flops 2147483648 | bytes 2097152 | tf_op jit(solution)/shard_map/flux_first/pallas_call | solution.py:639
  123.5 2.5 %all-to-all-done.6.values = bf16[16,32,128]{2,1,0:T(8,128)(2,1)S(1)} async-done(((bf16[16,32,128]{2,1,0:T(8,128)(2,1)}), bf16[16,32,128]{2,1,0:T(8,128)(2,1)S(1)}, u32[]{:S(2)}, u32[]{:S(2)}) %all-to-all-start.6) | async-done | bytes 131104 | tf_op jit(solution)/shard_map/all_to_all | solution.py:554
  126.0 0.0 copy-done.3
  126.0 0.0 copy-start.1
  126.0 2.2 %copy-done.1 = bf16[16,8,128,128]{3,2,1,0:T(8,128)(2,1)S(1)} copy-done((bf16[16,8,128,128]{3,2,1,0:T(8,128)(2,1)S(1)}, bf16[16,8,128,128]{3,2,1,0:T(8,128)(2,1)}, u32[]{:S(2)}) %copy-start.1) | copy-done | bytes 4194328
  128.3 0.0 copy-start.4
  128.3 0.7 copy-done.4
  129.0 2.6 %collect.3 = f32[16,8,128]{2,1,0:T(8,128)S(1)} custom-call(bf16[16,32,128]{2,1,0:T(8,128)(2,1)S(1)} %all-to-all-done.6.values, s32[8,16]{1,0:T(8,128)S(1)} %bitcast.6, bf16[16,8,128,128]{3,2,1,0:T(8,128)(2,1)S(1)} %copy-done.1, f32[8,128]{1,0:T(8,128)S(1)} %copy-done.4), custom_call_target="tpu_custom_call" | custom-call | flops 33554432 | bytes 4194304 | tf_op jit(solution)/shard_map/collect/pallas_call | solution.py:618
  131.5 10.0 %all_to_all.50 = f32[16,8,128]{2,1,0:T(8,128)S(1)} all-to-all(f32[16,8,128]{2,1,0:T(8,128)S(1)} %collect.3), channel_id=1, replica_groups=mesh['grp'=2,'tm'=16] {'tm'}, dimensions={0} | all-to-all | bytes 131072 | tf_op jit(solution)/shard_map/all_to_all | solution.py:554
  141.6 0.0 copy-start.7
  141.6 0.6 broadcast_in_dim.5
  142.2 3.5 %all-to-all-start.8 = ((f32[16,8,128]{2,1,0:T(8,128)}), f32[16,8,128]{2,1,0:T(8,128)S(1)}, u32[]{:S(2)}, u32[]{:S(2)}) async-start(f32[16,8,128]{2,1,0:T(8,128)} %broadcast_in_dim.5), calls=%async_computation.8 | async-start | bytes 131072 | tf_op jit(solution)/shard_map/all_to_all | solution.py:37
  145.7 0.0 all-gather.5.cloned.1.call-done.gathered
  145.8 0.0 copy-done.7
  145.8 6.4 %flux_second.1.flux_two = f32[1024,512]{1,0:T(8,128)} custom-call(f32[8,128]{1,0:T(8,128)} %copy-done.7, f32[8,2048]{1,0:T(8,128)} %get-tuple-element.18.time_part, f32[128,2048]{1,0:T(8,128)} %get-tuple-element.19.row_part, bf16[2048,512]{1,0:T(8,128)(2,1)} %all-gather.5.cloned.1.call-done.gathered), custom_call_target="tpu_custom_call" | custom-call | flops 2147483648 | bytes 2097152 | tf_op jit(solution)/shard_map/flux_second/pallas_call | solution.py:650
  152.2 0.4 all-to-all-done.8.image_in
  152.6 0.0 copy-start.6
  152.6 0.6 copy-done.6
  153.2 5.1 %last.1 = (f32[2,4,128]{2,1,0:T(4,128)}, f32[8,128,4,128]{3,2,1,0:T(4,128)}) custom-call(s32[1]{0:T(128)} %bitcast.me, f32[16,16,128]{2,1,0:T(8,128)} %all_to_all.45.everyone, f32[16,8,128]{2,1,0:T(8,128)} %copy-done.6, f32[16,8,128]{2,1,0:T(8,128)} %get-tuple-element.22.direction, f32[16,128]{1,0:T(8,128)} %get-tuple-element.17.sizes, ...), custom_call_target="tpu_custom_call" | custom-call | flops 1048576 | bytes 6291456 | tf_op jit(solution)/shard_map/last/pallas_call | solution.py:661
  (3 shorter events, 0.0 us)
Async XLA Ops:
  7.2 109.1 %all-gather.3.cloned.1.call-start = ((), (), s32[]{:S(2)}) async-start(), calls=%async_computation.9 | async-start | bytes 2228224 | tf_op jit(solution)/shard_map/all_gather | solution.py:570
  29.6 13.4 %all-to-all-start.1 = ((bf16[16,32,128]{2,1,0:T(8,128)(2,1)}), bf16[16,32,128]{2,1,0:T(8,128)(2,1)S(1)}, u32[]{:S(2)}, u32[]{:S(2)}) async-start(bf16[16,32,128]{2,1,0:T(8,128)(2,1)} %get-tuple-element.14), calls=%async_computation.1 | async-start | bytes 262144 | tf_op jit(solution)/shard_map/all_to_all | solution.py:554
  33.1 112.7 %all-gather.5.cloned.1.call-start = ((), (), s32[]{:S(2)}) async-start(), calls=%async_computation.10 | async-start | bytes 2228224 | tf_op jit(solution)/shard_map/all_gather | solution.py:638
  42.9 0.6 copy-start.5
  43.6 21.3 %copy-start = (bf16[16,8,128,128]{3,2,1,0:T(8,128)(2,1)S(1)}, bf16[16,8,128,128]{3,2,1,0:T(8,128)(2,1)}, u32[]{:S(2)}) copy-start(bf16[16,8,128,128]{3,2,1,0:T(8,128)(2,1)} %footprint.7) | copy-start | bytes 12582916
  43.6 21.3 %copy-start.2 = (s32[16,8]{0,1:T(8,128)S(1)}, s32[16,8]{0,1:T(8,128)}, u32[]{:S(2)}) copy-start(s32[16,8]{0,1:T(8,128)} %param.11) | copy-start | bytes 1540
  112.5 13.5 %all-to-all-start.6 = ((bf16[16,32,128]{2,1,0:T(8,128)(2,1)}), bf16[16,32,128]{2,1,0:T(8,128)(2,1)S(1)}, u32[]{:S(2)}, u32[]{:S(2)}) async-start(bf16[16,32,128]{2,1,0:T(8,128)(2,1)} %mix_columns.3), calls=%async_computation.6 | async-start | bytes 262144 | tf_op jit(solution)/shard_map/all_to_all | solution.py:554
  116.2 9.8 %copy-start.3 = (s32[16,8]{0,1:T(8,128)S(1)}, s32[16,8]{0,1:T(8,128)}, u32[]{:S(2)}) copy-start(s32[16,8]{0,1:T(8,128)} %param.11) | copy-start | bytes 1540
  126.0 2.2 %copy-start.1 = (bf16[16,8,128,128]{3,2,1,0:T(8,128)(2,1)S(1)}, bf16[16,8,128,128]{3,2,1,0:T(8,128)(2,1)}, u32[]{:S(2)}) copy-start(bf16[16,8,128,128]{3,2,1,0:T(8,128)(2,1)} %footprint.7) | copy-start | bytes 12582916
  128.3 0.7 copy-start.4
  141.6 4.2 %copy-start.7 = (f32[8,128]{1,0:T(8,128)}, f32[8,128]{1,0:T(8,128)S(1)}, u32[]{:S(2)}) copy-start(f32[8,128]{1,0:T(8,128)S(1)} %reduce_sum.19.after) | copy-start | bytes 12292
  142.2 10.4 %all-to-all-start.8 = ((f32[16,8,128]{2,1,0:T(8,128)}), f32[16,8,128]{2,1,0:T(8,128)S(1)}, u32[]{:S(2)}, u32[]{:S(2)}) async-start(f32[16,8,128]{2,1,0:T(8,128)} %broadcast_in_dim.5), calls=%async_computation.8 | async-start | bytes 131072 | tf_op jit(solution)/shard_map/all_to_all | solution.py:37
  152.6 0.6 copy-start.6
Sparse Core Ops, SparseCore 0:
  29.7 40.4 all-gather.2
  93.7 41.0 all-gather.4
where the time goes:
time: 166 us; the launch traced here: 165 us
  blocking collectives  75.2 us (45%)
  Pallas kernels  57.1 us (34%)
  between operations  14.2 us (9%)
  starting transfers between devices  10.8 us (7%)
  local copies, waits for them, and re-layouts  4.87 us (3%)
  waiting for transfers between devices  3.05 us (2%)
    all_to_all x5, blocking collectives, exchange(): return lax.all_to_all(array, 'tm', split_axis=0, concat_axis=0, tiled=True)  65 us
    pallas_call x2, Pallas kernels, prior(): call(mix_body, [vmem, hbm], column_shape, [pltpu.VMEM((width, every_tile)...  11.1 us
    all_to_all x1, blocking collectives, to_all(): return lax.all_to_all(copies, 'tm', split_axis=0, concat_axis=0, tiled=True)  10.2 us
    pallas_call x1, Pallas kernels, by_columns(): pl.pallas_call(build_body, grid=(8,), in_specs=[smem, whole(everyone.shap...  9.78 us
    pallas_call x1, Pallas kernels, by_columns(): call(flux_first_body, [vmem, vmem, hbm, hbm], [field_shape, shape_of((8,...  7.23 us
    all_to_all x2, starting transfers between devices, exchange(): return lax.all_to_all(array, 'tm', split_axis=0, concat_axis=0, tiled=True)  7.22 us
    pallas_call x1, Pallas kernels, by_columns(): call(flux_second_body, [hbm, vmem, hbm, hbm], field_shape, row_scratch +...  6.38 us
    pallas_call x1, Pallas kernels, by_columns(): call(update_body, [vmem] * 4 + [hbm], [column_shape, tile_shape, vector_s...  5.44 us
  transfers between devices with their start and end apart: 5, of which 2 were waited for; matrix products, arithmetic and copies ran while one was open for 0% of the time, Pallas kernels for 27%

commit v1 on v0

--- a/solution.py
+++ b/solution.py
@@ -254,18 +254,16 @@
         copies[d] = copies[0]
 
 
-def spread_tiles(vectors, held, copies, products, split):
-    owners, slots = held.shape[:2]
+def spread_tiles(vectors, footprint, products, split):
+    owners, slots = footprint.shape[:2]
     for owner in range(owners):
-        if owner % (owners // PIECES) == 0:
-            copies[owner // (owners // PIECES)].wait()
         rows = vectors[owner, 0:8]
         lhs = rows.astype(jnp.bfloat16)
         if split:
             upper = lhs.astype(jnp.float32)
             lhs = jnp.concatenate([upper, rows - upper], axis=0).astype(jnp.bfloat16)
         for c in range(slots):
-            r = jnp.dot(lhs, held[owner, c], preferred_element_type=jnp.float32)
+            r = jnp.dot(lhs, footprint[owner, c], preferred_element_type=jnp.float32)
             products[owner * slots + c] = r[:8] + r[8:] if split else r
 
 
@@ -282,11 +280,8 @@
         by_column[k * chunks : (k + 1) * chunks] = turned.reshape(chunks, width, LON)
 
 
-def first_body(
-    everyone, tile_block, lon, footprint, by_column, by_tile, products, held, arrived
-):
-    copies = fetch(footprint, held, arrived)
-    spread_tiles(everyone, held, copies, products, False)
+def first_body(everyone, tile_block, lon, footprint, by_column, by_tile, products):
+    spread_tiles(everyone, footprint, products, False)
     spread_end(products, second_of(tile_block), lon, by_column, by_tile)
 
 
@@ -309,9 +304,8 @@
 
 def update_body(
     everyone, image_in, tile_block, lon, footprint,
-    by_column, by_tile, direction, sizes, norm, products, held, arrived,
+    by_column, by_tile, direction, sizes, norm, products,
 ):
-    copies = fetch(footprint, held, arrived)
     first = everyone[:, 0:8, :]
     image = with_variance(image_in[...], everyone, first)
     norm_now = row_gram(first, first)
@@ -322,71 +316,83 @@
     direction[...] = residual + row_combine(first, row_weights(ratio))
     keep(sizes, step_size)
     keep(norm, norm_next)
-    spread_tiles(direction, held, copies, products, True)
+    spread_tiles(direction, footprint, products, True)
     spread_end(products, second_of(tile_block), lon, by_column, by_tile)
 
 
 def build_body(
-    me, everyone, time_cov, lat_cov, tile_prior, time_part, row_part, hot, cols, times
+    me, everyone, time_cov, lat_cov,
+    tile_prior, second_prior, time_part, row_part, hot, cols, times, sent,
 ):
     devices, tiles = everyone.shape[0], everyone.shape[2]
     steps_here = time_part.shape[0]
-    rows = tile_prior.shape[0]
-    step = pl.program_id(0)
-
-    @pl.when(step == 0)
-    def _():
-        at = lax.broadcasted_iota(jnp.int32, (LAT, tiles), 0)
-        for kind, cov in ((0, time_cov), (1, lat_cov)):
-            whole_cov = cov[...]
-            upper = whole_cov.astype(jnp.bfloat16)
-            lower = (whole_cov - upper.astype(jnp.float32)).astype(jnp.bfloat16)
-            ones = []
-            for d in range(devices):
-                place = (everyone[d, 10:11, :] + 0.5).astype(jnp.int32)
-                where = place // LAT + steps_here * d if kind == 0 else place % LAT
-                one = (at == where).astype(jnp.float32)
-                ones.append(one.astype(jnp.bfloat16))
-                turned = one.T.astype(jnp.bfloat16)
-                here = slice(d * tiles, (d + 1) * tiles)
-                hot[kind, here, 0:LAT] = turned
-                hot[kind, here, LAT : 2 * LAT] = turned
-            picked = jnp.dot(
-                jnp.concatenate([upper, lower], axis=0),
-                jnp.concatenate(ones, axis=1),
-                preferred_element_type=jnp.float32,
-            )
-            cols[kind] = picked.astype(jnp.bfloat16)
-            both = picked[:LAT] + picked[LAT:]
-            if kind == 0:
-                times[...] = both
-                mine = pl.ds(pl.multiple_of(me[0] * steps_here, steps_here), steps_here)
-                time_part[...] = times[mine, :]
-            else:
-                row_part[...] = both
-
-    block = pl.ds(pl.multiple_of(step * rows, rows), rows)
-    by_time = jnp.dot(hot[0, block, :], cols[0], preferred_element_type=jnp.float32)
-    by_row = jnp.dot(hot[1, block, :], cols[1], preferred_element_type=jnp.float32)
-    tile_prior[...] = (by_time * by_row).astype(jnp.bfloat16)
-
-
-def mix_body(columns, tile_prior, mixed, total, held, arrived):
-    copies = fetch(tile_prior, held, arrived)
+    at = lax.broadcasted_iota(jnp.int32, (LAT, tiles), 0)
+    for kind, cov in ((0, time_cov), (1, lat_cov)):
+        whole_cov = cov[...]
+        upper = whole_cov.astype(jnp.bfloat16)
+        lower = (whole_cov - upper.astype(jnp.float32)).astype(jnp.bfloat16)
+        ones = []
+        for d in range(devices):
+            place = (everyone[d, 10:11, :] + 0.5).astype(jnp.int32)
+            where = place // LAT + steps_here * d if kind == 0 else place % LAT
+            one = (at == where).astype(jnp.float32)
+            ones.append(one.astype(jnp.bfloat16))
+            turned = one.T.astype(jnp.bfloat16)
+            here = slice(d * tiles, (d + 1) * tiles)
+            hot[kind, here, 0:LAT] = turned
+            hot[kind, here, LAT : 2 * LAT] = turned
+        picked = jnp.dot(
+            jnp.concatenate([upper, lower], axis=0),
+            jnp.concatenate(ones, axis=1),
+            preferred_element_type=jnp.float32,
+        )
+        cols[kind] = picked.astype(jnp.bfloat16)
+        both = picked[:LAT] + picked[LAT:]
+        if kind == 0:
+            times[...] = both
+            mine = pl.ds(pl.multiple_of(me[0] * steps_here, steps_here), steps_here)
+            time_part[...] = times[mine, :]
+        else:
+            row_part[...] = both
+
+    rows = tile_prior.shape[0] // PIECES
+
+    def sending(piece):
+        block = pl.ds(pl.multiple_of(piece * rows, rows), rows)
+        return pltpu.make_async_copy(
+            tile_prior.at[block], second_prior.at[block], sent.at[piece]
+        )
+
+    @pl.loop(0, PIECES)
+    def _(piece):
+        block = pl.ds(pl.multiple_of(piece * rows, rows), rows)
+        by_time = jnp.dot(hot[0, block, :], cols[0], preferred_element_type=jnp.float32)
+        by_row = jnp.dot(hot[1, block, :], cols[1], preferred_element_type=jnp.float32)
+        tile_prior[block, :] = (by_time * by_row).astype(jnp.bfloat16)
+        sending(piece).start()
+
+    for piece in range(PIECES):
+        sending(piece).wait()
+
+
+def mix_body(columns, tile_prior, mixed):
     devices, width, tiles = columns.shape
-    part = devices // len(copies)
-    for p, copy in enumerate(copies):
-        at = range(p * part, (p + 1) * part)
-        lhs = jnp.concatenate([columns[d] for d in at], axis=1)
-        copy.wait()
+    lhs = jnp.concatenate([columns[d] for d in range(devices)], axis=1)
+    part = 512
+    for p in range(devices * tiles // part):
         product = jnp.dot(
-            lhs,
-            held[p * part * tiles : (p + 1) * part * tiles],
-            preferred_element_type=jnp.float32,
-        )
-        total[...] = product if p == 0 else total[...] + product
-    for d in range(devices):
-        mixed[d] = total[:, d * tiles : (d + 1) * tiles].astype(jnp.bfloat16)
+            lhs, tile_prior[:, p * part : (p + 1) * part], preferred_element_type=jnp.float32
+        )
+        for q in range(part // tiles):
+            piece = product[:, q * tiles : (q + 1) * tiles]
+            mixed[p * (part // tiles) + q] = piece.astype(jnp.bfloat16)
+
+
+def sum_body(terms, total, copies):
+    value = jnp.sum(terms[...], axis=0)
+    total[...] = value
+    for d in range(copies.shape[0]):
+        copies[d] = value
 
 
 def collect_body(values, tile_block, footprint, *rest):
@@ -491,7 +497,7 @@
 MIB = 1024 * 1024
 
 
-def params(grant=59):
+def params(grant=32):
     return pltpu.CompilerParams(vmem_limit_bytes=grant * MIB)
 
 
@@ -529,15 +535,11 @@
     row_scratch = [pltpu.VMEM(row_shape.shape, f32)]
     held_scratch = [pltpu.VMEM((every_tile, columns), bf16)]
     copied = [pltpu.SemaphoreType.DMA((1,)), pltpu.SemaphoreType.DMA((PIECES,))]
-    tile_scratch = [
-        pltpu.VMEM((tiles, 8, LON), f32),
-        pltpu.VMEM(footprint.shape, bf16),
-        pltpu.SemaphoreType.DMA((PIECES,)),
-    ]
+    tile_scratch = [pltpu.VMEM((tiles, 8, LON), f32)]
     tile_cost = cost(2 * 8 * footprint.size, footprint.size * 2)
     flux_cost = cost(2 * rows_here * every_tile * columns, every_tile * columns * 2)
 
-    def call(body, in_specs, out_shape, scratch, estimate, name, grant=59):
+    def call(body, in_specs, out_shape, scratch, estimate, name, grant=32):
         specs = [vmem] * len(out_shape) if isinstance(out_shape, list) else vmem
         return pl.pallas_call(
             body,
@@ -555,13 +557,13 @@
 
     packed_shape = shape_of((devices, 16, 128), f32)
     everyone = exchange(
-        call(pack_body, [vmem] * 3, packed_shape, [], cost(0, 1 << 17), "pack")(
+        call(pack_body, [vmem] * 3, packed_shape, [], cost(0, 12 * MIB), "pack")(
             right_sides, obs_var, tile_place.T
         )
     )
     by_column, by_tile = call(
         first_body,
-        [vmem, vmem, vmem, hbm],
+        [vmem] * 4,
         [column_shape, tile_shape],
         tile_scratch,
         tile_cost,
@@ -569,23 +571,14 @@
     )(everyone, turned_block, lon_cov, footprint)
     gathered_one = lax.all_gather(by_tile, "tm", axis=0, tiled=True)
 
-    build_rows = every_tile // 8
-    tile_prior, time_part, row_part = pl.pallas_call(
+    prior_shape = shape_of((every_tile, every_tile), bf16)
+    first_prior, second_prior, time_part, row_part = pl.pallas_call(
         build_body,
-        grid=(8,),
-        in_specs=[
-            smem,
-            whole(everyone.shape),
-            whole(time_cov.shape),
-            whole(lat_cov.shape),
-        ],
-        out_specs=[
-            pl.BlockSpec((build_rows, every_tile), lambda i: (i, 0)),
-            whole((steps_here, every_tile)),
-            whole(row_shape.shape),
-        ],
+        in_specs=[smem] + [vmem] * 3,
+        out_specs=[vmem, hbm, vmem, vmem],
         out_shape=[
-            shape_of((every_tile, every_tile), bf16),
+            prior_shape,
+            prior_shape,
             shape_of((steps_here, every_tile), f32),
             row_shape,
         ],
@@ -593,22 +586,19 @@
             pltpu.VMEM((2, every_tile, 2 * LAT), bf16),
             pltpu.VMEM((2, 2 * LAT, every_tile), bf16),
             pltpu.VMEM((LAT, every_tile), f32),
+            pltpu.SemaphoreType.DMA((PIECES,)),
         ],
-        compiler_params=params(),
+        compiler_params=params(40),
         cost_estimate=cost(4 * every_tile * every_tile * 256, every_tile * every_tile * 2),
         name="build_prior",
     )(me, everyone, time_cov, lat_cov)
 
-    def prior(by_column):
+    def prior(by_column, tile_prior):
         mixed = call(
             mix_body,
-            [vmem, hbm],
+            [vmem] * 2,
             column_shape,
-            [
-                pltpu.VMEM((width, every_tile), f32),
-                pltpu.VMEM((every_tile, every_tile), bf16),
-                pltpu.SemaphoreType.DMA((PIECES,)),
-            ],
+            [],
             cost(2 * width * every_tile**2, every_tile**2 * 2),
             "mix_columns",
         )(exchange(by_column), tile_prior)
@@ -619,20 +609,28 @@
             collect_body,
             [vmem] * 3 + [hbm] * len(after),
             vector_shape,
-            tile_scratch[:1],
+            tile_scratch,
             tile_cost,
             "collect",
-            48,
         )(values, turned_block, footprint, *after)
-        return exchange(sums).sum(0)
-
-    image = to_all(collect(prior(by_column)))
+        own, copies = call(
+            sum_body,
+            [vmem],
+            [shape_of((8, BLOCK_OBS), f32), vector_shape],
+            [],
+            cost(0, 12 * MIB),
+            "sum_terms",
+        )(exchange(sums))
+        return own, exchange(copies)
+
+
+    _, image = collect(prior(by_column, first_prior))
     by_column, by_tile, direction, sizes, norm = call(
         update_body,
-        [vmem] * 4 + [hbm],
+        [vmem] * 5,
         [column_shape, tile_shape, vector_shape, small_shape, small_shape],
         tile_scratch,
-        tile_cost,
+        cost(2 * 8 * footprint.size, 24 * MIB),
         "update_spread",
     )(everyone, image, turned_block, lon_cov, footprint)
     gathered_two = lax.all_gather(by_tile, "tm", axis=0, tiled=True)
@@ -645,8 +643,7 @@
         "flux_first",
     )(sizes, time_part, row_part, gathered_one)
 
-    own_image = collect(prior(by_column), token)
-    image = to_all(own_image)
+    own_image, image = collect(prior(by_column, second_prior), token)
     flux_two = call(
         flux_second_body,
         [hbm, vmem, hbm, hbm],

time: 166 us -> 160 us (0.964)
  Pallas kernels: 57.1 us -> 33.4 us
  local copies, waits for them, and re-layouts: 4.87 us -> 26.4 us
  blocking collectives: 75.2 us -> 72.3 us
    unnamed x16 -> x44, local copies, waits for them, and re-layouts: 4.22 us -> 26.4 us
    pallas_call x6 -> x8, Pallas kernels: 33.2 us -> 18.3 us  [the longest x1 8.03 us: by_columns(): pl.pallas_call(build_body, in_specs=[smem] + [vmem] * 3, out_specs=[vmem,...]
    all_to_all x1 -> x0, blocking collectives: 10.2 us -> none  [to_all(): return lax.all_to_all(copies, 'tm', split_axis=0, concat_axis=0, tiled=True)]
    all_to_all x5 -> x6, blocking collectives: 65 us -> 72.3 us  [exchange(): return lax.all_to_all(array, 'tm', split_axis=0, concat_axis=0, tiled=True)]
    pallas_call x1, Pallas kernels: 6.38 us -> 2.64 us  [by_columns(): call(flux_second_body, [hbm, vmem, hbm, hbm], field_shape, row_scratch +...]
    all_to_all x1 -> x0, starting transfers between devices: 3.5 us -> none  [to_all(): return lax.all_to_all(copies, 'tm', split_axis=0, concat_axis=0, tiled=True)]
    all_to_all x2 -> x3, starting transfers between devices: 7.22 us -> 10.7 us  [exchange(): return lax.all_to_all(array, 'tm', split_axis=0, concat_axis=0, tiled=True)]
    pallas_call x1, Pallas kernels: 7.23 us -> 4.29 us  [by_columns(): call(flux_first_body, [vmem, vmem, hbm, hbm], [field_shape, shape_of((8,...]
  transfers between devices with their start and end apart: 5 -> 5, of which waited for: 2 -> 2; matrix products, arithmetic and copies ran while one was open for 0% -> 0% of each run, Pallas kernels for 27% -> 17%
where the time goes in v1:
time: 160 us; the launch traced here: 159 us
  blocking collectives  72.3 us (45%)
  Pallas kernels  33.4 us (21%)
  local copies, waits for them, and re-layouts  26.4 us (16%)
  between operations  14.2 us (9%)
  starting transfers between devices  10.8 us (7%)
    all_to_all x6, blocking collectives, exchange(): return lax.all_to_all(array, 'tm', split_axis=0, concat_axis=0, tiled=True)  72.3 us
    unnamed x44, local copies, waits for them, and re-layouts  26.4 us
    all_to_all x3, starting transfers between devices, exchange(): return lax.all_to_all(array, 'tm', split_axis=0, concat_axis=0, tiled=True)  10.7 us
    pallas_call x1, Pallas kernels, by_columns(): pl.pallas_call(build_body, in_specs=[smem] + [vmem] * 3, out_specs=[vmem,...  8.03 us
    pallas_call x2, Pallas kernels, collect(): call(collect_body, [vmem] * 3 + [hbm] * len(after), vector_shape, tile_sc...  5.14 us
    pallas_call x1, Pallas kernels, by_columns(): call(flux_first_body, [vmem, vmem, hbm, hbm], [field_shape, shape_of((8,...  4.29 us
    pallas_call x2, Pallas kernels, prior(): call(mix_body, [vmem] * 2, column_shape, [], cost(2 * width * every_tile...  3.71 us
  transfers between devices with their start and end apart: 5, of which 2 were waited for; matrix products, arithmetic and copies ran while one was open for 0% of the time, Pallas kernels for 17%

profile of v1, /device:TPU:0, one launch (start us, length us, event | category | flops | bytes accessed | tf_op | source)
XLA Modules:
  0.0 158.6 jit_solution(10459550398842397909)
XLA Ops:
  7.2 0.0 all-gather.3.cloned.1.call-start
  7.2 0.0 copy-start.12
  7.2 0.7 copy-done.12
  7.9 0.0 copy-start.13
  7.9 0.7 copy-done.13
  8.6 0.0 copy-start.14
  8.6 0.7 copy-done.14
  9.3 0.1 pack.1
  9.4 15.1 %all_to_all.45.everyone = f32[16,16,128]{2,1,0:T(8,128)S(1)} all-to-all(f32[16,16,128]{2,1,0:T(8,128)S(1)} %pack.1), channel_id=1, replica_groups=mesh['grp'=2,'tm'=16] {'tm'}, dimensions={0} | all-to-all | bytes 262144 | tf_op jit(solution)/shard_map/all_to_all | solution.py:556
  24.5 0.0 copy-start
  24.5 2.2 %copy-done = bf16[16,8,128,128]{3,2,1,0:T(8,128)(2,1)S(1)} copy-done((bf16[16,8,128,128]{3,2,1,0:T(8,128)(2,1)S(1)}, bf16[16,8,128,128]{3,2,1,0:T(8,128)(2,1)}, u32[]{:S(2)}) %copy-start) | copy-done | bytes 4194328
  26.7 0.0 copy-start.8
  26.7 0.8 copy-done.8
  27.6 0.0 copy-start.10
  27.6 0.7 copy-done.10
  28.2 0.0 copy-start.17
  28.3 2.5 %spread_first.1 = (bf16[16,32,128]{2,1,0:T(8,128)(2,1)}, bf16[128,512]{1,0:T(8,128)(2,1)}) custom-call(f32[16,16,128]{2,1,0:T(8,128)S(1)} %all_to_all.45.everyone, s32[8,16]{1,0:T(8,128)S(1)} %bitcast.3, f32[128,128]{1,0:T(8,128)S(1)} %copy-done.8, bf16[16,8,128,128]{3,2,1,0:T(8,128)(2,1)S(1)} %copy-done), custom_call_target="tpu_custom_call" | custom-call | flops 33554432 | bytes 4194304 | tf_op jit(solution)/shard_map/spread_first/pallas_call | solution.py:564
  30.7 0.0 all-gather.3.cloned.1.call-update
  30.8 3.5 %all-to-all-start.1 = ((bf16[16,32,128]{2,1,0:T(8,128)(2,1)}), bf16[16,32,128]{2,1,0:T(8,128)(2,1)S(1)}, u32[]{:S(2)}, u32[]{:S(2)}) async-start(bf16[16,32,128]{2,1,0:T(8,128)(2,1)} %get-tuple-element.18), calls=%async_computation.1 | async-start | bytes 262144 | tf_op jit(solution)/shard_map/all_to_all | solution.py:556
  34.3 0.0 all-gather.5.cloned.1.call-start
  34.3 0.0 copy-done.17
  34.4 0.0 copy-done.18
  34.4 8.0 %build_prior.1 = (bf16[2048,2048]{1,0:T(8,128)(2,1)S(1)}, bf16[2048,2048]{1,0:T(8,128)(2,1)}, f32[8,2048]{1,0:T(8,128)S(1)}, f32[128,2048]{1,0:T(8,128)S(1)}) custom-call(s32[1]{0:T(128)} %bitcast.me, f32[16,16,128]{2,1,0:T(8,128)S(1)} %all_to_all.45.everyone, f32[128,128]{1,0:T(8,128)S(1)} %copy-done.17, f32[128,128]{1,0:T(8,128)S(1)} %copy-done.18), custom_call_target="tpu_custom_call" | custom-call | flops 4294967296 | bytes 8388608 | tf_op jit(solution)/shard_map/build_prior/pallas_call | solution.py:575
  42.4 0.0 copy-start.4
  42.4 3.2 %copy-done.4 = bf16[2048,2048]{1,0:T(8,128)(2,1)} copy-done((bf16[2048,2048]{1,0:T(8,128)(2,1)}, bf16[2048,2048]{1,0:T(8,128)(2,1)S(1)}, u32[]{:S(2)}) %copy-start.4) | copy-done | bytes 8388632
  45.7 0.6 copy-done.19
  46.3 0.0 all-to-all-done.1.columns
  46.3 3.4 %copy-done.5 = bf16[2048,2048]{1,0:T(8,128)(2,1)S(1)} copy-done((bf16[2048,2048]{1,0:T(8,128)(2,1)S(1)}, bf16[2048,2048]{1,0:T(8,128)(2,1)}, u32[]{:S(2)}) %copy-start.5) | copy-done | bytes 8388632
  49.7 1.5 mix_columns.2
  51.2 15.2 %all_to_all.46.values = bf16[16,32,128]{2,1,0:T(8,128)(2,1)S(1)} all-to-all(bf16[16,32,128]{2,1,0:T(8,128)(2,1)S(1)} %mix_columns.2), channel_id=1, replica_groups=mesh['grp'=2,'tm'=16] {'tm'}, dimensions={0} | all-to-all | bytes 262144 | tf_op jit(solution)/shard_map/all_to_all | solution.py:556
  66.3 0.0 copy-done.1
  66.4 0.0 copy-done.11
  66.4 2.6 %collect.2 = f32[16,8,128]{2,1,0:T(8,128)S(1)} custom-call(bf16[16,32,128]{2,1,0:T(8,128)(2,1)S(1)} %all_to_all.46.values, s32[8,16]{1,0:T(8,128)S(1)} %bitcast.4, bf16[16,8,128,128]{3,2,1,0:T(8,128)(2,1)S(1)} %copy-done.1), custom_call_target="tpu_custom_call" | custom-call | flops 33554432 | bytes 4194304 | tf_op jit(solution)/shard_map/collect/pallas_call | solution.py:608
  68.9 10.6 %all_to_all.47.terms = f32[16,8,128]{2,1,0:T(8,128)S(1)} all-to-all(f32[16,8,128]{2,1,0:T(8,128)S(1)} %collect.2), channel_id=1, replica_groups=mesh['grp'=2,'tm'=16] {'tm'}, dimensions={0} | all-to-all | bytes 131072 | tf_op jit(solution)/shard_map/all_to_all | solution.py:556
  79.5 0.6 sum_terms.2
  80.1 9.5 %all_to_all.48.image_in = f32[16,8,128]{2,1,0:T(8,128)S(1)} all-to-all(f32[16,8,128]{2,1,0:T(8,128)S(1)} %get-tuple-element.20), channel_id=1, replica_groups=mesh['grp'=2,'tm'=16] {'tm'}, dimensions={0} | all-to-all | bytes 131072 | tf_op jit(solution)/shard_map/all_to_all | solution.py:556
  89.6 0.0 copy-done.9
  89.6 2.7 %update_spread.1 = (bf16[16,32,128]{2,1,0:T(8,128)(2,1)S(1)}, bf16[128,512]{1,0:T(8,128)(2,1)}, f32[16,8,128]{2,1,0:T(8,128)S(1)}, f32[16,128]{1,0:T(8,128)S(1)}, f32[16,128]{1,0:T(8,128)S(1)}) custom-call(f32[16,16,128]{2,1,0:T(8,128)S(1)} %all_to_all.45.everyone, f32[16,8,128]{2,1,0:T(8,128)S(1)} %all_to_all.48.image_in, s32[8,16]{1,0:T(8,128)S(1)} %bitcast.5, ...), custom_call_target="tpu_custom_call" | custom-call | flops 33554432 | bytes 25165824 | tf_op jit(solution)/shard_map/update_spread/pallas_call | solution.py:628
  92.3 0.0 all-gather.5.cloned.1.call-update
  92.3 10.6 %all_to_all.49.columns = bf16[16,32,128]{2,1,0:T(8,128)(2,1)S(1)} all-to-all(bf16[16,32,128]{2,1,0:T(8,128)(2,1)S(1)} %get-tuple-element.21), channel_id=1, replica_groups=mesh['grp'=2,'tm'=16] {'tm'}, dimensions={0} | all-to-all | bytes 262144 | tf_op jit(solution)/shard_map/all_to_all | solution.py:556
  102.8 3.4 %copy-done.3 = bf16[2048,2048]{1,0:T(8,128)(2,1)S(1)} copy-done((bf16[2048,2048]{1,0:T(8,128)(2,1)S(1)}, bf16[2048,2048]{1,0:T(8,128)(2,1)}, u32[]{:S(2)}) %copy-start.3) | copy-done | bytes 8388632
  106.2 2.2 %mix_columns.3 = bf16[16,32,128]{2,1,0:T(8,128)(2,1)} custom-call(bf16[16,32,128]{2,1,0:T(8,128)(2,1)S(1)} %all_to_all.49.columns, bf16[2048,2048]{1,0:T(8,128)(2,1)S(1)} %copy-done.3), custom_call_target="tpu_custom_call" | custom-call | flops 268435456 | bytes 8388608 | tf_op jit(solution)/shard_map/mix_columns/pallas_call | solution.py:597
  108.4 3.7 %all-to-all-start.6 = ((bf16[16,32,128]{2,1,0:T(8,128)(2,1)}), bf16[16,32,128]{2,1,0:T(8,128)(2,1)S(1)}, u32[]{:S(2)}, u32[]{:S(2)}) async-start(bf16[16,32,128]{2,1,0:T(8,128)(2,1)} %mix_columns.3), calls=%async_computation.6 | async-start | bytes 262144 | tf_op jit(solution)/shard_map/all_to_all | solution.py:556
  112.1 0.0 all-gather.3.cloned.1.call-done.gathered
  112.1 0.0 copy-start.15
  112.1 1.6 copy-done.15
  113.7 0.8 copy-done.20
  114.6 4.3 %flux_first.1 = (f32[1024,512]{1,0:T(8,128)S(1)}, f32[8,128]{1,0:T(8,128)S(1)}) custom-call(f32[16,128]{1,0:T(8,128)S(1)} %get-tuple-element.23.sizes, f32[8,2048]{1,0:T(8,128)S(1)} %copy-done.20, f32[128,2048]{1,0:T(8,128)S(1)} %get-tuple-element.25.row_part, bf16[2048,512]{1,0:T(8,128)(2,1)S(1)} %copy-done.15), custom_call_target="tpu_custom_call" | custom-call | flops 2147483648 | bytes 2097152 | tf_op jit(solution)/shard_map/flux_first/pallas_call | solution.py:637
  118.9 1.0 all-to-all-done.6.values
  119.9 2.2 %copy-done.2 = bf16[16,8,128,128]{3,2,1,0:T(8,128)(2,1)S(1)} copy-done((bf16[16,8,128,128]{3,2,1,0:T(8,128)(2,1)S(1)}, bf16[16,8,128,128]{3,2,1,0:T(8,128)(2,1)}, u32[]{:S(2)}) %copy-start.2) | copy-done | bytes 4194328
  122.1 2.6 %collect.3 = f32[16,8,128]{2,1,0:T(8,128)S(1)} custom-call(bf16[16,32,128]{2,1,0:T(8,128)(2,1)S(1)} %all-to-all-done.6.values, s32[8,16]{1,0:T(8,128)S(1)} %bitcast.6, bf16[16,8,128,128]{3,2,1,0:T(8,128)(2,1)S(1)} %copy-done.2, f32[8,128]{1,0:T(8,128)S(1)} %get-tuple-element.27.rest_0_), custom_call_target="tpu_custom_call" | custom-call | flops 33554432 | bytes 4194304 | tf_op jit(solution)/shard_map/collect/pallas_call | solution.py:608
  124.7 11.5 %all_to_all.50.terms = f32[16,8,128]{2,1,0:T(8,128)S(1)} all-to-all(f32[16,8,128]{2,1,0:T(8,128)S(1)} %collect.3), channel_id=1, replica_groups=mesh['grp'=2,'tm'=16] {'tm'}, dimensions={0} | all-to-all | bytes 131072 | tf_op jit(solution)/shard_map/all_to_all | solution.py:556
  136.2 0.6 sum_terms.3
  136.8 3.5 %all-to-all-start.8 = ((f32[16,8,128]{2,1,0:T(8,128)}), f32[16,8,128]{2,1,0:T(8,128)S(1)}, u32[]{:S(2)}, u32[]{:S(2)}) async-start(f32[16,8,128]{2,1,0:T(8,128)} %get-tuple-element.28), calls=%async_computation.8 | async-start | bytes 131072 | tf_op jit(solution)/shard_map/all_to_all | solution.py:556
  140.3 0.0 all-gather.5.cloned.1.call-done.gathered
  140.3 0.0 copy-start.16
  140.3 1.6 copy-done.16
  141.9 0.8 copy-done.21
  142.8 2.6 %flux_second.1.flux_two = f32[1024,512]{1,0:T(8,128)S(1)} custom-call(f32[8,128]{1,0:T(8,128)S(1)} %get-tuple-element.32.after, f32[8,2048]{1,0:T(8,128)S(1)} %copy-done.21, f32[128,2048]{1,0:T(8,128)S(1)} %get-tuple-element.25.row_part, bf16[2048,512]{1,0:T(8,128)(2,1)S(1)} %copy-done.16), custom_call_target="tpu_custom_call" | custom-call | flops 2147483648 | bytes 2097152 | tf_op jit(solution)/shard_map/flux_second/pallas_call | solution.py:647
  145.4 0.0 copy-start.6
  145.4 1.3 copy-done.6
  146.7 0.4 all-to-all-done.8.image_in
  147.2 1.6 %copy-done.7 = f32[1024,512]{1,0:T(8,128)S(1)} copy-done((f32[1024,512]{1,0:T(8,128)S(1)}, f32[1024,512]{1,0:T(8,128)}, u32[]{:S(2)}) %copy-start.7) | copy-done | bytes 2097176
  148.7 3.1 %last.1 = (f32[2,4,128]{2,1,0:T(4,128)}, f32[8,128,4,128]{3,2,1,0:T(4,128)}) custom-call(s32[1]{0:T(128)} %bitcast.me, f32[16,16,128]{2,1,0:T(8,128)S(1)} %all_to_all.45.everyone, f32[16,8,128]{2,1,0:T(8,128)S(1)} %all-to-all-done.8.image_in, f32[16,8,128]{2,1,0:T(8,128)S(1)} %get-tuple-element.29.direction, f32[16,128]{1,0:T(8,128)S(1)} %get-tuple-element.23.sizes, ...), custom_call_target="tpu_custom_call" | custom-call | flops 1048576 | bytes 6291456 | tf_op jit(solution)/shard_map/last/pallas_call | solution.py:658
  (11 shorter events, 0.0 us)
Async XLA Ops:
  7.2 105.0 %all-gather.3.cloned.1.call-start = ((), (), s32[]{:S(2)}) async-start(), calls=%async_computation.9 | async-start | bytes 2228224 | tf_op jit(solution)/shard_map/all_gather | solution.py:572
  7.2 0.7 copy-start.12
  7.9 0.7 copy-start.13
  8.6 0.7 copy-start.14
  24.5 2.2 %copy-start = (bf16[16,8,128,128]{3,2,1,0:T(8,128)(2,1)S(1)}, bf16[16,8,128,128]{3,2,1,0:T(8,128)(2,1)}, u32[]{:S(2)}) copy-start(bf16[16,8,128,128]{3,2,1,0:T(8,128)(2,1)} %footprint.7) | copy-start | bytes 12582916
  26.7 0.8 copy-start.8
  27.6 0.7 copy-start.10
  28.2 6.1 %copy-start.17 = (f32[128,128]{1,0:T(8,128)S(1)}, f32[128,128]{1,0:T(8,128)}, u32[]{:S(2)}) copy-start(f32[128,128]{1,0:T(8,128)} %time_cov.1) | copy-start | bytes 196612
  28.2 6.1 %copy-start.18 = (f32[128,128]{1,0:T(8,128)S(1)}, f32[128,128]{1,0:T(8,128)}, u32[]{:S(2)}) copy-start(f32[128,128]{1,0:T(8,128)} %lat_cov.1) | copy-start | bytes 196612
  30.8 15.5 %all-to-all-start.1 = ((bf16[16,32,128]{2,1,0:T(8,128)(2,1)}), bf16[16,32,128]{2,1,0:T(8,128)(2,1)S(1)}, u32[]{:S(2)}, u32[]{:S(2)}) async-start(bf16[16,32,128]{2,1,0:T(8,128)(2,1)} %get-tuple-element.18), calls=%async_computation.1 | async-start | bytes 262144 | tf_op jit(solution)/shard_map/all_to_all | solution.py:556
  34.3 106.0 %all-gather.5.cloned.1.call-start = ((), (), s32[]{:S(2)}) async-start(), calls=%async_computation.10 | async-start | bytes 2228224 | tf_op jit(solution)/shard_map/all_gather | solution.py:636
  42.4 3.2 %copy-start.4 = (bf16[2048,2048]{1,0:T(8,128)(2,1)}, bf16[2048,2048]{1,0:T(8,128)(2,1)S(1)}, u32[]{:S(2)}) copy-start(bf16[2048,2048]{1,0:T(8,128)(2,1)S(1)} %get-tuple-element.19.tile_prior) | copy-start | bytes 25165828
  45.6 0.6 copy-start.19
  46.3 3.4 %copy-start.5 = (bf16[2048,2048]{1,0:T(8,128)(2,1)S(1)}, bf16[2048,2048]{1,0:T(8,128)(2,1)}, u32[]{:S(2)}) copy-start(bf16[2048,2048]{1,0:T(8,128)(2,1)} %copy-done.4) | copy-start | bytes 25165828
  49.7 16.7 %copy-start.1 = (bf16[16,8,128,128]{3,2,1,0:T(8,128)(2,1)S(1)}, bf16[16,8,128,128]{3,2,1,0:T(8,128)(2,1)}, u32[]{:S(2)}) copy-start(bf16[16,8,128,128]{3,2,1,0:T(8,128)(2,1)} %footprint.7) | copy-start | bytes 12582916
  49.7 16.7 %copy-start.11 = (s32[16,8]{0,1:T(8,128)S(1)}, s32[16,8]{0,1:T(8,128)}, u32[]{:S(2)}) copy-start(s32[16,8]{0,1:T(8,128)} %param.11) | copy-start | bytes 1540
  66.4 23.2 %copy-start.9 = (f32[128,128]{1,0:T(8,128)S(1)}, f32[128,128]{1,0:T(8,128)}, u32[]{:S(2)}) copy-start(f32[128,128]{1,0:T(8,128)} %lon.3) | copy-start | bytes 196612
  102.8 3.4 %copy-start.3 = (bf16[2048,2048]{1,0:T(8,128)(2,1)S(1)}, bf16[2048,2048]{1,0:T(8,128)(2,1)}, u32[]{:S(2)}) copy-start(bf16[2048,2048]{1,0:T(8,128)(2,1)} %get-tuple-element.22.tile_prior) | copy-start | bytes 25165828
  108.4 11.5 %all-to-all-start.6 = ((bf16[16,32,128]{2,1,0:T(8,128)(2,1)}), bf16[16,32,128]{2,1,0:T(8,128)(2,1)S(1)}, u32[]{:S(2)}, u32[]{:S(2)}) async-start(bf16[16,32,128]{2,1,0:T(8,128)(2,1)} %mix_columns.3), calls=%async_computation.6 | async-start | bytes 262144 | tf_op jit(solution)/shard_map/all_to_all | solution.py:556
  112.1 1.6 %copy-start.15 = (bf16[2048,512]{1,0:T(8,128)(2,1)S(1)}, bf16[2048,512]{1,0:T(8,128)(2,1)}, u32[]{:S(2)}) copy-start(bf16[2048,512]{1,0:T(8,128)(2,1)} %all-gather.3.cloned.1.call-done.gathered) | copy-start | bytes 6291460
  113.7 0.8 copy-start.20
  119.9 2.2 %copy-start.2 = (bf16[16,8,128,128]{3,2,1,0:T(8,128)(2,1)S(1)}, bf16[16,8,128,128]{3,2,1,0:T(8,128)(2,1)}, u32[]{:S(2)}) copy-start(bf16[16,8,128,128]{3,2,1,0:T(8,128)(2,1)} %footprint.7) | copy-start | bytes 12582916
  136.8 10.3 %all-to-all-start.8 = ((f32[16,8,128]{2,1,0:T(8,128)}), f32[16,8,128]{2,1,0:T(8,128)S(1)}, u32[]{:S(2)}, u32[]{:S(2)}) async-start(f32[16,8,128]{2,1,0:T(8,128)} %get-tuple-element.28), calls=%async_computation.8 | async-start | bytes 131072 | tf_op jit(solution)/shard_map/all_to_all | solution.py:556
  140.3 1.6 %copy-start.16 = (bf16[2048,512]{1,0:T(8,128)(2,1)S(1)}, bf16[2048,512]{1,0:T(8,128)(2,1)}, u32[]{:S(2)}) copy-start(bf16[2048,512]{1,0:T(8,128)(2,1)} %all-gather.5.cloned.1.call-done.gathered) | copy-start | bytes 6291460
  141.9 0.8 copy-start.21
  145.4 1.3 copy-start.6
  147.2 1.6 %copy-start.7 = (f32[1024,512]{1,0:T(8,128)S(1)}, f32[1024,512]{1,0:T(8,128)}, u32[]{:S(2)}) copy-start(f32[1024,512]{1,0:T(8,128)} %copy-done.6) | copy-start | bytes 6291460
Sparse Core Ops, SparseCore 0:
  30.9 40.1 all-gather.2
  92.4 39.1 all-gather.4
